TPU v7x, 128 devices: a whole 4x4x4 slice. The times are simulated.
128 devices in a mesh: shot: 4 (over z_lo, core), sub: 32 (over y, z_hi, x).
Axes of the slice: x: 4, y: 4, z: 4 (z_hi: 2, z_lo: 2; z = z_hi * 2 + z_lo), core: 2. Of those that a mesh axis runs over, the one named last changes fastest.
Arguments:
- courant_tiles: float32 [768, 6, 64, 128], P(('shot', 'sub')), may hold values from 0.2 to 0.44
- tile_place: int32 [64, 12], replicated, may hold values from 0 to 11, each once within a row
- anchors: int32 [4, 2], replicated, may hold values from 0 to 32, as said below
- source_cells: int32 [4, 3], replicated, may hold values from 0 to 383, as said below
- wavelet: float32 [4, 4], P('shot'), may hold values from -6 to 6
- forward_state: float32 [4, 2, 192, 384, 128], P('shot', None, 'sub'), may hold values from -1.75 to 1.75
- adjoint_state: float32 [4, 2, 192, 384, 128], P('shot', None, 'sub'), may hold values from -1.75 to 1.75
- residual: float32 [4, 4, 192, 384], P('shot', None, 'sub'), may hold values from -1.75 to 1.75
Outputs:
- forward_out: float32 [4, 2, 192, 384, 128], P('shot', None, 'sub')
- adjoint_out: float32 [4, 2, 192, 384, 128], P('shot', None, 'sub')
- gradient_tiles: float32 [768, 6, 64, 128], P(('shot', 'sub'))
Inputs may be any that keep to these rules, and one draw needn't show every extreme that they name: `anchors`: the first entry is 0 to 32, the second 0 to 6, so that an aperture lies inside the model; some shot's aperture lies at the far end of the first dimension (first entry 32), another's at the anchor. `source_cells`: entries are below 192, 384 and 128 for the three dimensions; some shot's source lies at the aperture's far corner, another's on the plane where the third entry is 0. `tile_place`: each row lists every place 0 to 11 once.
All inputs are finite; a program needn't handle non-finite values.
Results may differ from a plain program's by a relative error of at most 0.00024.
Values sent between devices are 32-bit elements; how exact they have to be, the bound alone decides.
No kernel may reach another device: no remote copies, remote signals or barrier semaphores. Data moves between devices by JAX's collectives and lax.ppermute only.
A program may use at most 128 MiB of HBM per device.

v0:
```python
import jax
import jax.numpy as jnp
from jax import lax
from jax.sharding import PartitionSpec as P

KY = 6
STEPS = 4


WEIGHTS = (1.6, -0.2, 8.0 / 315.0, -1.0 / 560.0)
CENTER = -205.0 / 72.0 * 3.0


def from_behind(value, axis, steps):
    count = lax.axis_size(axis)
    pairs = [(source, (source + steps) % count) for source in range(count)]
    return lax.ppermute(value, axis, pairs)


def extended_2(block, sides, width):
    for axis, dim in sides:
        count = lax.axis_size(axis)
        forward = [(i, i + 1) for i in range(count - 1)]
        backward = [(target, source) for source, target in forward]
        low = lax.ppermute(
            lax.slice_in_dim(block, block.shape[dim] - width, None, axis=dim), axis, forward
        )
        high = lax.ppermute(lax.slice_in_dim(block, 0, width, axis=dim), axis, backward)
        block = jnp.concatenate([low, block, high], axis=dim)
    return block


def stencil(padded):
    size_x = padded.shape[0] - 8
    size_y = padded.shape[1] - 8
    size_z = padded.shape[2] - 8
    summed = CENTER * padded[4 : 4 + size_x, 4 : 4 + size_y, 4 : 4 + size_z]
    for distance, weight in enumerate(WEIGHTS, 1):
        summed = summed + weight * (
            padded[4 + distance : 4 + distance + size_x, 4 : 4 + size_y, 4 : 4 + size_z]
            + padded[4 - distance : 4 - distance + size_x, 4 : 4 + size_y, 4 : 4 + size_z]
        )
    for distance, weight in enumerate(WEIGHTS, 1):
        summed = summed + weight * (
            padded[4 : 4 + size_x, 4 + distance : 4 + distance + size_y, 4 : 4 + size_z]
            + padded[4 : 4 + size_x, 4 - distance : 4 - distance + size_y, 4 : 4 + size_z]
        )
    for distance, weight in enumerate(WEIGHTS, 1):
        summed = summed + weight * (
            padded[4 : 4 + size_x, 4 : 4 + size_y, 4 + distance : 4 + distance + size_z]
            + padded[4 : 4 + size_x, 4 : 4 + size_y, 4 - distance : 4 - distance + size_z]
        )
    return summed


def pad_sides(extended):
    return jnp.pad(extended, ((0, 0), (4, 4), (4, 4)))


def body(
    courant_tiles,
    tile_place,
    anchors,
    source_cells,
    wavelet,
    forward_state,
    adjoint_state,
    residual,
):
    shot_count = lax.axis_size("shot")
    sub_count = lax.axis_size("sub")
    my_shot = lax.axis_index("shot")
    my_sub = lax.axis_index("sub")
    held_tiles = courant_tiles.shape[0]
    share_size = held_tiles // 2
    tile_x, tile_y, depth = (courant_tiles.shape[1], courant_tiles.shape[2], courant_tiles.shape[3])
    need_index = jnp.arange(KY, dtype=jnp.int32)
    start_x = anchors[:, 0]
    start_y = anchors[:, 1]
    column = jnp.where(my_sub >= start_x, my_sub, my_sub + sub_count)
    upper_half = (my_sub < start_x).astype(jnp.int32)
    inside_ids = start_y[:, None] + need_index[None, :]
    places = tile_place[column[:, None], inside_ids]
    own_places = places[my_shot]
    own_upper = upper_half[my_shot]
    gathered = lax.all_gather(courant_tiles, "shot", axis=0, tiled=True)
    gathered_rows = (
        own_places // share_size * held_tiles + own_upper * share_size + own_places % share_size
    )
    column_part = gathered[gathered_rows]
    bit_total = sub_count.bit_length() - 1
    amount = anchors[my_shot, 0] % sub_count
    moving = column_part
    for bit_level in range(bit_total):
        shifted = from_behind(moving, "sub", sub_count - (1 << bit_level))
        moving = jnp.where(amount >> bit_level & 1 == 1, shifted, moving)
    courant = moving.transpose(1, 0, 2, 3).reshape(tile_x, KY * tile_y, depth)
    weight_sq = courant * courant
    cells = source_cells[my_shot]
    local_x = cells[0] - my_sub * tile_x
    shape = courant.shape
    source_mask = (
        (lax.broadcasted_iota(jnp.int32, shape, 0) == local_x)
        & (lax.broadcasted_iota(jnp.int32, shape, 1) == cells[1])
        & (lax.broadcasted_iota(jnp.int32, shape, 2) == cells[2])
    ).astype(jnp.float32)
    previous = forward_state[0, 0]
    current = forward_state[0, 1]
    adjoint_old = adjoint_state[0, 0]
    adjoint_now = adjoint_state[0, 1]
    curvatures = []
    kept = []
    for step in range(STEPS):
        extended = extended_2(current, (("sub", 0),), 4)
        curvature = stencil(pad_sides(extended))
        advanced = 2.0 * current - previous + weight_sq * curvature
        advanced = advanced + source_mask * wavelet[0, step]
        curvatures.append(curvature)
        previous, current = (current, advanced)
    for step in range(STEPS):
        kept.append(adjoint_now)
        extended = extended_2(weight_sq * adjoint_now, (("sub", 0),), 4)
        adjoint_next = 2.0 * adjoint_now - adjoint_old + stencil(pad_sides(extended))
        adjoint_next = adjoint_next.at[:, :, 0].add(residual[0, step])
        adjoint_old, adjoint_now = (adjoint_now, adjoint_next)
    imaging = jnp.zeros(shape, jnp.float32)
    for step in range(STEPS):
        imaging = imaging + kept[step] * curvatures[STEPS - 1 - step]
    gradient_slab = 2.0 * courant * imaging
    gradient_parts = gradient_slab.reshape(tile_x, KY, tile_y, depth).transpose(1, 0, 2, 3)
    returning = gradient_parts
    for bit_level in range(bit_total):
        shifted = from_behind(returning, "sub", 1 << bit_level)
        returning = jnp.where(amount >> bit_level & 1 == 1, shifted, returning)
    flat_parts = returning.reshape(KY, tile_x * tile_y * depth)
    store_rows = (
        own_places // share_size * held_tiles + own_upper * share_size + own_places % share_size
    )
    store_table = (
        store_rows[None, :] == jnp.arange(shot_count * held_tiles, dtype=jnp.int32)[:, None]
    ).astype(jnp.float32)
    spread = jnp.dot(
        store_table, flat_parts, precision=lax.Precision.HIGHEST, preferred_element_type=jnp.float32
    ).reshape(shot_count * held_tiles, tile_x, tile_y, depth)
    gradient_tiles = lax.psum_scatter(spread, "shot", scatter_dimension=0, tiled=True)
    forward_out = jnp.stack([previous, current])[None]
    adjoint_out = jnp.stack([adjoint_old, adjoint_now])[None]
    return (forward_out, adjoint_out, gradient_tiles)


def solution(mesh):
    return jax.shard_map(
        body,
        mesh=mesh,
        in_specs=(
            P(("shot", "sub"), None, None, None),
            P(),
            P(),
            P(),
            P("shot", None),
            P("shot", None, "sub", None, None),
            P("shot", None, "sub", None, None),
            P("shot", None, "sub", None),
        ),
        out_specs=(
            P("shot", None, "sub", None, None),
            P("shot", None, "sub", None, None),
            P(("shot", "sub"), None, None, None),
        ),
        check_vma=False,
    )
```

profile of v0, /device:TPU:1, one launch (start us, length us, event | category | flops | bytes accessed | tf_op | source)
XLA Modules:
  0.0 721.7 jit_solution(3315640259135708689)
XLA Ops:
  10.4 53.9 %all-gather.2.cloned.1.call-done = f32[24,6,64,128]{3,2,1,0:T(8,128)} async-done(((f32[6,6,64,128]{3,2,1,0:T(8,128)}), f32[24,6,64,128]{3,2,1,0:T(8,128)}) %all-gather.2.cloned.1.call-update) | async-done | bytes 4718608 | tf_op jit(solution)/shard_map/all_gather | solution.py:86
  67.3 6.9 collective-permute-start
  76.2 23.7 %collective-permute-done = f32[6,6,64,128]{3,2,1,0:T(8,128)S(1)} collective-permute-done((f32[6,6,64,128]{3,2,1,0:T(8,128)S(1)}, f32[6,6,64,128]{3,2,1,0:T(8,128)S(1)}, u32[]{:S(2)}, u32[]{:S(2)}) %collective-permute-start) | collective-permute-done | bytes 1179680 | tf_op jit(solution)/shard_map/ppermute | solution.py:17
  102.7 26.1 %collective-permute-done.1 = f32[6,6,64,128]{3,2,1,0:T(8,128)S(1)} collective-permute-done((f32[6,6,64,128]{3,2,1,0:T(8,128)S(1)}, f32[6,6,64,128]{3,2,1,0:T(8,128)S(1)}, u32[]{:S(2)}, u32[]{:S(2)}) %collective-permute-start.1) | collective-permute-done | bytes 1179680 | tf_op jit(solution)/shard_map/ppermute | solution.py:17
  130.0 26.8 %collective-permute-done.2 = f32[6,6,64,128]{3,2,1,0:T(8,128)} collective-permute-done((f32[6,6,64,128]{3,2,1,0:T(8,128)S(1)}, f32[6,6,64,128]{3,2,1,0:T(8,128)}, u32[]{:S(2)}, u32[]{:S(2)}) %collective-permute-start.2) | collective-permute-done | bytes 1179680 | tf_op jit(solution)/shard_map/ppermute | solution.py:17
  161.4 7.7 %collective-permute-start.6 = (f32[4,384,128]{2,1,0:T(8,128)}, f32[4,384,128]{2,1,0:T(8,128)}, u32[]{:S(2)}, u32[]{:S(2)}) collective-permute-start(f32[4,384,128]{2,1,0:T(8,128)} %get-tuple-element.68), channel_id=1, source_target_pairs={{0,1},{1,2},{2,3},{3,4},{4,5},{5,6},{6,7},{7,8},{8,9},{9,10},{10,1... | collective-permute-start | bytes 2359304 | tf_op jit(solution)/shard_map/ppermute | solution.py:25
  187.3 5.7 select_maximum_fusion.14
  193.0 17.3 %collective-permute-done.4 = f32[6,6,64,128]{3,2,1,0:T(8,128)S(1)} collective-permute-done((f32[6,6,64,128]{3,2,1,0:T(8,128)S(1)}, f32[6,6,64,128]{3,2,1,0:T(8,128)S(1)}, u32[]{:S(2)}, u32[]{:S(2)}) %collective-permute-start.4) | collective-permute-done | bytes 1179680 | tf_op jit(solution)/shard_map/ppermute | solution.py:17
  214.7 7.1 collective-permute-start.14
  223.1 25.4 %fusion.284 = (f32[6,384,128]{2,1,0:T(8,128)S(1)}, f32[6,384,128]{2,1,0:T(8,128)}) fusion(f32[6,6,64,128]{3,2,1,0:T(8,128)S(1)} %copy.43, f32[1,2,6,384,128]{4,3,2,1,0:T(8,128)} %param.21, f32[]{:T(128)} %bitcast.17, pred[128]{0:T(512)(128)(4,1)S(1)} %iota_compare_fusion.6, pred[384]{0:T(512)(128)(4,1)S(1)} %iota_compare_fusion.5, ...), kind=kLoop, calls=%fused_computation.502 | loop fusion | flops 15630336 | bytes 27525642 | tf_op jit(solution)/shard_map/add | solution.py:117
  253.9 6.0 collective-permute-start.8
  259.9 5.3 select_maximum_fusion.6
  265.2 24.7 %fusion.91 = f32[6,384,128]{2,1,0:T(8,128)S(1)} fusion(f32[6,384,128]{2,1,0:T(8,128)} %copy-done.17, f32[4,384,128]{2,1,0:T(8,128)} %collective-permute-done.14, f32[4,384,128]{2,1,0:T(8,128)} %collective-permute-done.13, f32[14,392,136]{2,1,0:T(8,128)} %select_maximum_fusion.6, f32[1,2,6,384,128]{4,3,2,1,0:T(8,128)} %param.22), kind=kLoop, calls=%fused_computation.212 | loop fusion | flops 14155776 | bytes 25165824 | tf_op jit(solution)/shard_map/add | solution.py:123
  297.5 20.6 %collective-permute-start.16 = (f32[4,384,128]{2,1,0:T(8,128)}, f32[4,384,128]{2,1,0:T(8,128)}, u32[]{:S(2)}, u32[]{:S(2)}) collective-permute-start(f32[4,384,128]{2,1,0:T(8,128)} %get-tuple-element.85), channel_id=1, source_target_pairs={{0,1},{1,2},{2,3},{3,4},{4,5},{5,6},{6,7},{7,8},{8,9},{9,10},{10,1... | collective-permute-start | bytes 2359304 | tf_op jit(solution)/shard_map/ppermute | solution.py:25
  319.4 5.3 select_maximum_fusion.12
  324.7 24.9 %fusion.286 = (f32[6,384,128]{2,1,0:T(8,128)S(1)}, f32[6,384,128]{2,1,0:T(8,128)}) fusion(f32[6,6,64,128]{3,2,1,0:T(8,128)S(1)} %copy.43, f32[6,384,128]{2,1,0:T(8,128)} %copy-done.9, f32[]{:T(128)} %bitcast.18, pred[128]{0:T(512)(128)(4,1)S(1)} %iota_compare_fusion.6, pred[384]{0:T(512)(128)(4,1)S(1)} %iota_compare_fusion.5, ...), kind=kLoop, calls=%fused_computation.504 | loop fusion | flops 15630336 | bytes 26345994 | tf_op jit(solution)/shard_map/add | solution.py:117
  352.5 5.7 collective-permute-start.10
  358.2 5.3 select_maximum_fusion.4
  363.5 24.9 %fusion.66 = f32[6,384,128]{2,1,0:T(8,128)S(1)} fusion(f32[6,384,128]{2,1,0:T(8,128)} %copy-done.15, f32[4,384,128]{2,1,0:T(8,128)} %collective-permute-done.16, f32[4,384,128]{2,1,0:T(8,128)} %collective-permute-done.15, f32[14,392,136]{2,1,0:T(8,128)} %select_maximum_fusion.4, f32[6,384,128]{2,1,0:T(8,128)S(1)} %scatter-add.14, ...), kind=kLoop, calls=%fused_computation.187 | loop fusion | flops 14155776 | bytes 25165824 | tf_op jit(solution)/shard_map/add | solution.py:123
  396.9 6.1 collective-permute-start.18
  409.6 24.3 %fusion.288 = (f32[6,384,128]{2,1,0:T(8,128)S(1)}, f32[6,384,128]{2,1,0:T(8,128)}) fusion(f32[6,6,64,128]{3,2,1,0:T(8,128)S(1)} %copy.43, f32[6,384,128]{2,1,0:T(8,128)} %copy-done.9, f32[6,384,128]{2,1,0:T(8,128)} %copy-done.7, f32[]{:T(128)} %bitcast.19, pred[128]{0:T(512)(128)(4,1)S(1)} %iota_compare_fusion.6, pred[384]{0:T(512)(128)(4,1)S(1)} %iota_compare_fusion.5, ...), kind=kLoop, calls=%fused_computation.506 | loop fusion | flops 15630336 | bytes 26345994 | tf_op jit(solution)/shard_map/add | solution.py:117
  436.4 5.7 collective-permute-start.12
  447.5 25.7 %fusion.41 = f32[6,384,128]{2,1,0:T(8,128)} fusion(f32[6,384,128]{2,1,0:T(8,128)} %copy-done.13, f32[4,384,128]{2,1,0:T(8,128)} %collective-permute-done.18, f32[4,384,128]{2,1,0:T(8,128)} %collective-permute-done.17, f32[14,392,136]{2,1,0:T(8,128)} %select_maximum_fusion.2, f32[6,384,128]{2,1,0:T(8,128)S(1)} %scatter-add.14, f32[6,384,128]{2,1,0:T(8,128)} %copy-done.2), kind=kLoop, calls=%fused_computation.162 | loop fusion | flops 14155776 | bytes 25165824 | tf_op jit(solution)/shard_map/add | solution.py:123
  483.3 8.2 %bitcast_multiply_fusion = (f32[6,384,128]{2,1,0:T(8,128)S(1)}, f32[6,384,128]{2,1,0:T(8,128)}) fusion(f32[6,6,64,128]{3,2,1,0:T(8,128)} %copy.49, f32[6,384,128]{2,1,0:T(8,128)S(1)} %copy-done.5, f32[6,384,128]{2,1,0:T(8,128)} %get-tuple-element.67, f32[6,384,128]{2,1,0:T(8,128)S(1)} %copy-done.3, f32[6,384,128]{2,1,0:T(8,128)} %get-tuple-element.65, ...), kind=kLoop, calls=%fused_computation.485 | loop fusion | flops 15630336 | bytes 33423360 | tf_op jit(solution)/shard_map/mul | solution.py:129
  495.0 17.6 %collective-permute-done.21 = f32[6,6,64,128]{3,2,1,0:T(8,128)S(1)} collective-permute-done((f32[6,6,64,128]{3,2,1,0:T(8,128)S(1)}, f32[6,6,64,128]{3,2,1,0:T(8,128)S(1)}, u32[]{:S(2)}, u32[]{:S(2)}) %collective-permute-start.21) | collective-permute-done | bytes 1179680 | tf_op jit(solution)/shard_map/ppermute | solution.py:17
  512.7 6.4 collective-permute-start.22
  519.1 27.4 %collective-permute-done.22 = f32[6,6,64,128]{3,2,1,0:T(8,128)S(1)} collective-permute-done((f32[6,6,64,128]{3,2,1,0:T(8,128)S(1)}, f32[6,6,64,128]{3,2,1,0:T(8,128)S(1)}, u32[]{:S(2)}, u32[]{:S(2)}) %collective-permute-start.22) | collective-permute-done | bytes 1179680 | tf_op jit(solution)/shard_map/ppermute | solution.py:17
  546.8 34.4 %collective-permute-done.23 = f32[6,6,64,128]{3,2,1,0:T(8,128)S(1)} collective-permute-done((f32[6,6,64,128]{3,2,1,0:T(8,128)S(1)}, f32[6,6,64,128]{3,2,1,0:T(8,128)S(1)}, u32[]{:S(2)}, u32[]{:S(2)}) %collective-permute-start.23) | collective-permute-done | bytes 1179680 | tf_op jit(solution)/shard_map/ppermute | solution.py:17
  581.5 17.2 %collective-permute-done.24 = f32[6,6,64,128]{3,2,1,0:T(8,128)S(1)} collective-permute-done((f32[6,6,64,128]{3,2,1,0:T(8,128)S(1)}, f32[6,6,64,128]{3,2,1,0:T(8,128)S(1)}, u32[]{:S(2)}, u32[]{:S(2)}) %collective-permute-start.24) | collective-permute-done | bytes 1179680 | tf_op jit(solution)/shard_map/ppermute | solution.py:17
  600.5 26.7 %collective-permute-done.25 = f32[6,6,64,128]{3,2,1,0:T(8,128)S(1)} collective-permute-done((f32[6,6,64,128]{3,2,1,0:T(8,128)S(1)}, f32[6,6,64,128]{3,2,1,0:T(8,128)S(1)}, u32[]{:S(2)}, u32[]{:S(2)}) %collective-permute-start.25) | collective-permute-done | bytes 1179680 | tf_op jit(solution)/shard_map/ppermute | solution.py:17
  660.6 22.7 %fusion.16 = f32[6,384,128]{2,1,0:T(8,128)} fusion(f32[6,384,128]{2,1,0:T(8,128)S(1)} %copy-done.12, f32[4,384,128]{2,1,0:T(8,128)} %collective-permute-done.20, f32[4,384,128]{2,1,0:T(8,128)} %collective-permute-done.19, f32[14,392,136]{2,1,0:T(8,128)} %select_maximum_fusion, f32[6,384,128]{2,1,0:T(8,128)S(1)} %copy-done.4, f32[6,384,128]{2,1,0:T(8,128)S(1)} %copy-done.6), kind=kLoop, calls=%fused_computation.137 | loop fusion | flops 14155776 | bytes 25165824 | tf_op jit(solution)/shard_map/add | solution.py:123
  689.2 25.3 %reduce-scatter.2.cloned.1.call-done = f32[6,6,64,128]{3,2,1,0:T(8,128)} async-done(((f32[24,6,64,128]{3,2,1,0:T(8,128)}), f32[6,6,64,128]{3,2,1,0:T(8,128)}) %reduce-scatter.2.cloned.1.call-update) | async-done | bytes 1179664 | tf_op jit(solution)/shard_map/reduce_scatter | solution.py:145
  (155 shorter events, 133.3 us)
Async XLA Ops:
  7.2 57.1 %all-gather.2.cloned.1.call-start = ((), (), s32[]{:S(2)}) async-start(), calls=%async_computation.1 | async-start | bytes 5898240 | tf_op jit(solution)/shard_map/all_gather | solution.py:86
  7.9 706.5 %reduce-scatter.2.cloned.1.call-start = ((), (), s32[]{:S(2)}) async-start(), calls=%async_computation.2 | async-start | bytes 5898240 | tf_op jit(solution)/shard_map/reduce_scatter | solution.py:145
  67.3 32.6 %collective-permute-start = (f32[6,6,64,128]{3,2,1,0:T(8,128)S(1)}, f32[6,6,64,128]{3,2,1,0:T(8,128)S(1)}, u32[]{:S(2)}, u32[]{:S(2)}) collective-permute-start(f32[6,6,64,128]{3,2,1,0:T(8,128)S(1)} %gather_fusion.1), channel_id=1, source_target_pairs={{0,31},{1,0},{2,1},{3,2},{4,3},{5,4},{6,5},{7,6},{8,7},{9,8},{10,9... | collective-permute-start | bytes 3538952 | tf_op jit(solution)/shard_map/ppermute | solution.py:17
  100.1 28.6 %collective-permute-start.1 = (f32[6,6,64,128]{3,2,1,0:T(8,128)S(1)}, f32[6,6,64,128]{3,2,1,0:T(8,128)S(1)}, u32[]{:S(2)}, u32[]{:S(2)}) collective-permute-start(f32[6,6,64,128]{3,2,1,0:T(8,128)S(1)} %broadcast_select_fusion.1), channel_id=1, source_target_pairs={{0,30},{1,31},{2,0},{3,1},{4,2},{5,3},{6,4},{7,5},{8,6},{9,7},{10,... | collective-permute-start | bytes 3538952 | tf_op jit(solution)/shard_map/ppermute | solution.py:17
  129.0 27.8 %collective-permute-start.2 = (f32[6,6,64,128]{3,2,1,0:T(8,128)S(1)}, f32[6,6,64,128]{3,2,1,0:T(8,128)}, u32[]{:S(2)}, u32[]{:S(2)}) collective-permute-start(f32[6,6,64,128]{3,2,1,0:T(8,128)S(1)} %broadcast_select_fusion.3), channel_id=1, source_target_pairs={{0,28},{1,29},{2,30},{3,31},{4,0},{5,1},{6,2},{7,3},{8,4},{9,5},{1... | collective-permute-start | bytes 3538952 | tf_op jit(solution)/shard_map/ppermute | solution.py:17
  130.0 28.9 %copy-start.18 = (f32[1,2,6,384,128]{4,3,2,1,0:T(8,128)S(1)}, f32[1,2,6,384,128]{4,3,2,1,0:T(8,128)}, u32[]{:S(2)}) copy-start(f32[1,2,6,384,128]{4,3,2,1,0:T(8,128)} %param.21) | copy-start | bytes 7077892
  158.3 25.4 %collective-permute-start.3 = (f32[6,6,64,128]{3,2,1,0:T(8,128)S(1)}, f32[6,6,64,128]{3,2,1,0:T(8,128)}, u32[]{:S(2)}, u32[]{:S(2)}) collective-permute-start(f32[6,6,64,128]{3,2,1,0:T(8,128)S(1)} %broadcast_select_fusion.5), channel_id=1, source_target_pairs={{0,24},{1,25},{2,26},{3,27},{4,28},{5,29},{6,30},{7,31},{8,0},{9,1... | collective-permute-start | bytes 3538952 | tf_op jit(solution)/shard_map/ppermute | solution.py:17
  160.1 27.2 %collective-permute-start.5 = (f32[4,384,128]{2,1,0:T(8,128)}, f32[4,384,128]{2,1,0:T(8,128)}, u32[]{:S(2)}, u32[]{:S(2)}) collective-permute-start(f32[4,384,128]{2,1,0:T(8,128)} %get-tuple-element.69), channel_id=1, source_target_pairs={{1,0},{2,1},{3,2},{4,3},{5,4},{6,5},{7,6},{8,7},{9,8},{10,9},{11,1... | collective-permute-start | bytes 2359304 | tf_op jit(solution)/shard_map/ppermute | solution.py:28
  161.4 25.9 %collective-permute-start.6 = (f32[4,384,128]{2,1,0:T(8,128)}, f32[4,384,128]{2,1,0:T(8,128)}, u32[]{:S(2)}, u32[]{:S(2)}) collective-permute-start(f32[4,384,128]{2,1,0:T(8,128)} %get-tuple-element.68), channel_id=1, source_target_pairs={{0,1},{1,2},{2,3},{3,4},{4,5},{5,6},{6,7},{7,8},{8,9},{9,10},{10,1... | collective-permute-start | bytes 2359304 | tf_op jit(solution)/shard_map/ppermute | solution.py:25
  183.9 26.4 %collective-permute-start.4 = (f32[6,6,64,128]{3,2,1,0:T(8,128)S(1)}, f32[6,6,64,128]{3,2,1,0:T(8,128)S(1)}, u32[]{:S(2)}, u32[]{:S(2)}) collective-permute-start(f32[6,6,64,128]{3,2,1,0:T(8,128)S(1)} %broadcast_select_fusion.7), channel_id=1, source_target_pairs={{0,16},{1,17},{2,18},{3,19},{4,20},{5,21},{6,22},{7,23},{8,24},{9,... | collective-permute-start | bytes 3538952 | tf_op jit(solution)/shard_map/ppermute | solution.py:17
  213.4 46.5 %copy-start.17 = (f32[6,384,128]{2,1,0:T(8,128)}, f32[6,384,128]{2,1,0:T(8,128)S(1)}, u32[]{:S(2)}) copy-start(f32[6,384,128]{2,1,0:T(8,128)S(1)} %bitcast_multiply_fusion.2) | copy-start | bytes 3538948
  214.7 45.1 %collective-permute-start.14 = (f32[4,384,128]{2,1,0:T(8,128)}, f32[4,384,128]{2,1,0:T(8,128)}, u32[]{:S(2)}, u32[]{:S(2)}) collective-permute-start(f32[4,384,128]{2,1,0:T(8,128)} %get-tuple-element.87), channel_id=1, source_target_pairs={{0,1},{1,2},{2,3},{3,4},{4,5},{5,6},{6,7},{7,8},{8,9},{9,10},{10,1... | collective-permute-start | bytes 2359304 | tf_op jit(solution)/shard_map/ppermute | solution.py:25
  221.8 38.1 %collective-permute-start.13 = (f32[4,384,128]{2,1,0:T(8,128)}, f32[4,384,128]{2,1,0:T(8,128)}, u32[]{:S(2)}, u32[]{:S(2)}) collective-permute-start(f32[4,384,128]{2,1,0:T(8,128)} %get-tuple-element.86), channel_id=1, source_target_pairs={{1,0},{2,1},{3,2},{4,3},{5,4},{6,5},{7,6},{8,7},{9,8},{10,9},{11,1... | collective-permute-start | bytes 2359304 | tf_op jit(solution)/shard_map/ppermute | solution.py:28
  248.5 70.9 %copy-start.9 = (f32[6,384,128]{2,1,0:T(8,128)}, f32[6,384,128]{2,1,0:T(8,128)S(1)}, u32[]{:S(2)}) copy-start(f32[6,384,128]{2,1,0:T(8,128)S(1)} %get-tuple-element.66) | copy-start | bytes 3538948
  252.6 66.8 %collective-permute-start.7 = (f32[4,384,128]{2,1,0:T(8,128)}, f32[4,384,128]{2,1,0:T(8,128)}, u32[]{:S(2)}, u32[]{:S(2)}) collective-permute-start(f32[4,384,128]{2,1,0:T(8,128)} %get-tuple-element.81), channel_id=1, source_target_pairs={{1,0},{2,1},{3,2},{4,3},{5,4},{6,5},{7,6},{8,7},{9,8},{10,9},{11,1... | collective-permute-start | bytes 2359304 | tf_op jit(solution)/shard_map/ppermute | solution.py:28
  253.9 65.5 %collective-permute-start.8 = (f32[4,384,128]{2,1,0:T(8,128)}, f32[4,384,128]{2,1,0:T(8,128)}, u32[]{:S(2)}, u32[]{:S(2)}) collective-permute-start(f32[4,384,128]{2,1,0:T(8,128)} %get-tuple-element.80), channel_id=1, source_target_pairs={{0,1},{1,2},{2,3},{3,4},{4,5},{5,6},{6,7},{7,8},{8,9},{9,10},{10,1... | collective-permute-start | bytes 2359304 | tf_op jit(solution)/shard_map/ppermute | solution.py:25
  297.5 60.7 %collective-permute-start.16 = (f32[4,384,128]{2,1,0:T(8,128)}, f32[4,384,128]{2,1,0:T(8,128)}, u32[]{:S(2)}, u32[]{:S(2)}) collective-permute-start(f32[4,384,128]{2,1,0:T(8,128)} %get-tuple-element.85), channel_id=1, source_target_pairs={{0,1},{1,2},{2,3},{3,4},{4,5},{5,6},{6,7},{7,8},{8,9},{9,10},{10,1... | collective-permute-start | bytes 2359304 | tf_op jit(solution)/shard_map/ppermute | solution.py:25
  318.1 40.1 %collective-permute-start.15 = (f32[4,384,128]{2,1,0:T(8,128)}, f32[4,384,128]{2,1,0:T(8,128)}, u32[]{:S(2)}, u32[]{:S(2)}) collective-permute-start(f32[4,384,128]{2,1,0:T(8,128)} %get-tuple-element.84), channel_id=1, source_target_pairs={{1,0},{2,1},{3,2},{4,3},{5,4},{6,5},{7,6},{8,7},{9,8},{10,9},{11,1... | collective-permute-start | bytes 2359304 | tf_op jit(solution)/shard_map/ppermute | solution.py:28
  351.2 53.1 %collective-permute-start.9 = (f32[4,384,128]{2,1,0:T(8,128)}, f32[4,384,128]{2,1,0:T(8,128)}, u32[]{:S(2)}, u32[]{:S(2)}) collective-permute-start(f32[4,384,128]{2,1,0:T(8,128)} %get-tuple-element.79), channel_id=1, source_target_pairs={{1,0},{2,1},{3,2},{4,3},{5,4},{6,5},{7,6},{8,7},{9,8},{10,9},{11,1... | collective-permute-start | bytes 2359304 | tf_op jit(solution)/shard_map/ppermute | solution.py:28
  352.5 51.8 %collective-permute-start.10 = (f32[4,384,128]{2,1,0:T(8,128)}, f32[4,384,128]{2,1,0:T(8,128)}, u32[]{:S(2)}, u32[]{:S(2)}) collective-permute-start(f32[4,384,128]{2,1,0:T(8,128)} %get-tuple-element.78), channel_id=1, source_target_pairs={{0,1},{1,2},{2,3},{3,4},{4,5},{5,6},{6,7},{7,8},{8,9},{9,10},{10,1... | collective-permute-start | bytes 2359304 | tf_op jit(solution)/shard_map/ppermute | solution.py:25
  396.9 45.3 %collective-permute-start.18 = (f32[4,384,128]{2,1,0:T(8,128)}, f32[4,384,128]{2,1,0:T(8,128)}, u32[]{:S(2)}, u32[]{:S(2)}) collective-permute-start(f32[4,384,128]{2,1,0:T(8,128)} %get-tuple-element.83), channel_id=1, source_target_pairs={{0,1},{1,2},{2,3},{3,4},{4,5},{5,6},{6,7},{7,8},{8,9},{9,10},{10,1... | collective-permute-start | bytes 2359304 | tf_op jit(solution)/shard_map/ppermute | solution.py:25
  403.0 39.2 %collective-permute-start.17 = (f32[4,384,128]{2,1,0:T(8,128)}, f32[4,384,128]{2,1,0:T(8,128)}, u32[]{:S(2)}, u32[]{:S(2)}) collective-permute-start(f32[4,384,128]{2,1,0:T(8,128)} %get-tuple-element.82), channel_id=1, source_target_pairs={{1,0},{2,1},{3,2},{4,3},{5,4},{6,5},{7,6},{8,7},{9,8},{10,9},{11,1... | collective-permute-start | bytes 2359304 | tf_op jit(solution)/shard_map/ppermute | solution.py:28
  435.2 44.2 %collective-permute-start.11 = (f32[4,384,128]{2,1,0:T(8,128)}, f32[4,384,128]{2,1,0:T(8,128)}, u32[]{:S(2)}, u32[]{:S(2)}) collective-permute-start(f32[4,384,128]{2,1,0:T(8,128)} %get-tuple-element.77), channel_id=1, source_target_pairs={{1,0},{2,1},{3,2},{4,3},{5,4},{6,5},{7,6},{8,7},{9,8},{10,9},{11,1... | collective-permute-start | bytes 2359304 | tf_op jit(solution)/shard_map/ppermute | solution.py:28
  436.4 42.9 %collective-permute-start.12 = (f32[4,384,128]{2,1,0:T(8,128)}, f32[4,384,128]{2,1,0:T(8,128)}, u32[]{:S(2)}, u32[]{:S(2)}) collective-permute-start(f32[4,384,128]{2,1,0:T(8,128)} %get-tuple-element.76), channel_id=1, source_target_pairs={{0,1},{1,2},{2,3},{3,4},{4,5},{5,6},{6,7},{7,8},{8,9},{9,10},{10,1... | collective-permute-start | bytes 2359304 | tf_op jit(solution)/shard_map/ppermute | solution.py:25
  491.6 21.0 %collective-permute-start.21 = (f32[6,6,64,128]{3,2,1,0:T(8,128)S(1)}, f32[6,6,64,128]{3,2,1,0:T(8,128)S(1)}, u32[]{:S(2)}, u32[]{:S(2)}) collective-permute-start(f32[6,6,64,128]{3,2,1,0:T(8,128)S(1)} %bitcast.148), channel_id=1, source_target_pairs={{0,1},{1,2},{2,3},{3,4},{4,5},{5,6},{6,7},{7,8},{8,9},{9,10},{10,1... | collective-permute-start | bytes 3538952 | tf_op jit(solution)/shard_map/ppermute | solution.py:17
  512.7 33.8 %collective-permute-start.22 = (f32[6,6,64,128]{3,2,1,0:T(8,128)S(1)}, f32[6,6,64,128]{3,2,1,0:T(8,128)S(1)}, u32[]{:S(2)}, u32[]{:S(2)}) collective-permute-start(f32[6,6,64,128]{3,2,1,0:T(8,128)S(1)} %broadcast_select_fusion), channel_id=1, source_target_pairs={{0,2},{1,3},{2,4},{3,5},{4,6},{5,7},{6,8},{7,9},{8,10},{9,11},{10,... | collective-permute-start | bytes 3538952 | tf_op jit(solution)/shard_map/ppermute | solution.py:17
  546.7 34.5 %collective-permute-start.23 = (f32[6,6,64,128]{3,2,1,0:T(8,128)S(1)}, f32[6,6,64,128]{3,2,1,0:T(8,128)S(1)}, u32[]{:S(2)}, u32[]{:S(2)}) collective-permute-start(f32[6,6,64,128]{3,2,1,0:T(8,128)S(1)} %broadcast_select_fusion.2), channel_id=1, source_target_pairs={{0,4},{1,5},{2,6},{3,7},{4,8},{5,9},{6,10},{7,11},{8,12},{9,13},{1... | collective-permute-start | bytes 3538952 | tf_op jit(solution)/shard_map/ppermute | solution.py:17
  581.4 17.3 %collective-permute-start.24 = (f32[6,6,64,128]{3,2,1,0:T(8,128)S(1)}, f32[6,6,64,128]{3,2,1,0:T(8,128)S(1)}, u32[]{:S(2)}, u32[]{:S(2)}) collective-permute-start(f32[6,6,64,128]{3,2,1,0:T(8,128)S(1)} %broadcast_select_fusion.4), channel_id=1, source_target_pairs={{0,8},{1,9},{2,10},{3,11},{4,12},{5,13},{6,14},{7,15},{8,16},{9,17... | collective-permute-start | bytes 3538952 | tf_op jit(solution)/shard_map/ppermute | solution.py:17
  598.9 28.3 %collective-permute-start.25 = (f32[6,6,64,128]{3,2,1,0:T(8,128)S(1)}, f32[6,6,64,128]{3,2,1,0:T(8,128)S(1)}, u32[]{:S(2)}, u32[]{:S(2)}) collective-permute-start(f32[6,6,64,128]{3,2,1,0:T(8,128)S(1)} %broadcast_select_fusion.6), channel_id=1, source_target_pairs={{0,16},{1,17},{2,18},{3,19},{4,20},{5,21},{6,22},{7,23},{8,24},{9,... | collective-permute-start | bytes 3538952 | tf_op jit(solution)/shard_map/ppermute | solution.py:17
  640.0 10.7 %collective-permute-start.20 = (f32[4,384,128]{2,1,0:T(8,128)}, f32[4,384,128]{2,1,0:T(8,128)}, u32[]{:S(2)}, u32[]{:S(2)}) collective-permute-start(f32[4,384,128]{2,1,0:T(8,128)} %get-tuple-element.73), channel_id=1, source_target_pairs={{0,1},{1,2},{2,3},{3,4},{4,5},{5,6},{6,7},{7,8},{8,9},{9,10},{10,1... | collective-permute-start | bytes 2359304 | tf_op jit(solution)/shard_map/ppermute | solution.py:25
  642.3 13.0 %collective-permute-start.19 = (f32[4,384,128]{2,1,0:T(8,128)}, f32[4,384,128]{2,1,0:T(8,128)}, u32[]{:S(2)}, u32[]{:S(2)}) collective-permute-start(f32[4,384,128]{2,1,0:T(8,128)} %get-tuple-element.72), channel_id=1, source_target_pairs={{1,0},{2,1},{3,2},{4,3},{5,4},{6,5},{7,6},{8,7},{9,8},{10,9},{11,1... | collective-permute-start | bytes 2359304 | tf_op jit(solution)/shard_map/ppermute | solution.py:28
  687.6 26.9 %copy-start.1 = (s32[64,12]{0,1:T(8,128)S(1)}, s32[64,12]{0,1:T(8,128)}, u32[]{:S(2)}) copy-start(s32[64,12]{0,1:T(8,128)} %param.17) | copy-start | bytes 9220
  (22 other events, 103.1 us)
Sparse Core Ops, SparseCore 0:
  9.7 54.5 all-gather.1
  633.5 80.8 reduce-scatter.1
where the time goes:
time: 736 us; the launch traced here: 722 us
  waiting for transfers between devices  308 us (42%)
  other arithmetic  247 us (34%)
  starting transfers between devices  96.2 us (13%)
  local copies, waits for them, and re-layouts  51.1 us (7%)
  between operations  17.7 us (2%)
    ppermute x10, waiting for transfers between devices, from_behind(): return lax.ppermute(value, axis, pairs)  220 us
    add x4, other arithmetic, body(): 2.0 * adjoint_now - adjoint_old + stencil(pad_sides(extended))  97.9 us
    add x3, other arithmetic, body(): advanced = advanced + source_mask * wavelet[0, step]  74.6 us
    ppermute x8, starting transfers between devices, extended_2(): lax.ppermute(lax.slice_in_dim(block, block.shape[dim] - width, None, axis...  61.2 us
    all_gather x1, waiting for transfers between devices, body(): gathered = lax.all_gather(courant_tiles, 'shot', axis=0, tiled=True)  53.9 us
    concatenate x8, other arithmetic, extended_2(): block = jnp.concatenate([low, block, high], axis=dim)  41.4 us
    reduce_scatter x1, waiting for transfers between devices, body(): lax.psum_scatter(spread, 'shot', scatter_dimension=0, tiled=True)  25.3 us
    ppermute x10, starting transfers between devices, from_behind(): return lax.ppermute(value, axis, pairs)  24.7 us
  transfers between devices with their start and end apart: 28, of which 14 were waited for; matrix products, arithmetic and copies ran while one was open for 37% of the time, Pallas kernels for 0%

commit v1 on v0

v1 whole, which is shorter than its diff:
```python
import functools

import jax
import jax.numpy as jnp
from jax import lax
from jax.experimental import pallas as pl
from jax.experimental.pallas import tpu as pltpu
from jax.sharding import PartitionSpec as P

CX = 6
TY = 64
AZ = 128
KY = 6
AY = KY * TY
STEPS = 4
N_SHOT = 4
N_SUB = 32
SHARE = 3
R = 4
PAD = 8

WEIGHTS = (1.6, -0.2, 8.0 / 315.0, -1.0 / 560.0)
CENTER = -205.0 / 72.0 * 3.0

F32 = jnp.float32
SLAB = (CX, AY, AZ)
HALO = (R, AY, AZ)
BLOCK = pl.BlockSpec((CX, TY, AZ), lambda i, *_: (0, i, 0))
HBLOCK = pl.BlockSpec((R, TY, AZ), lambda i, *_: (0, i, 0))
WHOLE = pl.BlockSpec(SLAB, lambda i, *_: (0, 0, 0))
VMEM = 40 * 1024 * 1024


def sds(shape):
    return jax.ShapeDtypeStruct(shape, F32)


def fill_pad(src, pad):
    @pl.when(pl.program_id(0) == 0)
    def _():
        pad[:, 0:PAD, :] = jnp.zeros((CX, PAD, AZ), F32)
        pad[:, PAD + AY :, :] = jnp.zeros((CX, PAD, AZ), F32)
        pad[:, PAD : PAD + AY, :] = src[...]


def laplacian(x, src, lo, hi, pad):
    base = pl.multiple_of(pl.program_id(0) * TY, TY)

    def plane(k):
        if k < 0:
            return lo[k + R]
        if k >= CX:
            return hi[k - CX]
        return src[k, pl.ds(base, TY), :]

    here = plane(x)
    lane = lax.broadcasted_iota(jnp.int32, (TY, AZ), 1)
    out = CENTER * here
    for r, w in enumerate(WEIGHTS, 1):
        out = out + w * (plane(x + r) + plane(x - r))
    for r, w in enumerate(WEIGHTS, 1):
        out = out + w * (
            pad[x, pl.ds(base + (PAD + r), TY), :] + pad[x, pl.ds(base + (PAD - r), TY), :]
        )
    for r, w in enumerate(WEIGHTS, 1):
        up = jnp.where(lane < AZ - r, pltpu.roll(here, AZ - r, 1), 0.0)
        down = jnp.where(lane >= r, pltpu.roll(here, r, 1), 0.0)
        out = out + w * (up + down)
    return out


def add_source(out, cells, amp, halos):
    col = cells[1] - pl.program_id(0) * TY
    inside = (cells[0] >= 0) & (cells[0] < CX) & (col >= 0) & (col < TY)

    @pl.when(inside)
    def _():
        lane = lax.broadcasted_iota(jnp.int32, (1, 1, AZ), 2)
        x = cells[0]
        row = out[pl.ds(x, 1), pl.ds(col, 1), :]
        out[pl.ds(x, 1), pl.ds(col, 1), :] = row + jnp.where(lane == cells[2], amp, 0.0)

    if halos is not None:
        halos[0][...] = out[0:R]
        halos[1][...] = out[CX - R :]


def lap_kernel(src, lo, hi, lap, pad):
    fill_pad(src, pad)
    for x in range(CX):
        lap[x] = laplacian(x, src, lo, hi, pad)


def first_kernel(cells, amps, p0, pm, lap, c, q, p1, plo, phi, u, ulo, uhi):
    for x in range(CX):
        wsq = c[x] * c[x]
        p1[x] = 2.0 * p0[x] - pm[x] + wsq * lap[x]
        u[x] = wsq * q[x]
    ulo[...] = u[0:R]
    uhi[...] = u[CX - R :]
    add_source(p1, cells, amps[0], (plo, phi))


def forward_kernel(step, cells, amps, src, lo, hi, old, c, lap, new, nlo, nhi, pad):
    fill_pad(src, pad)
    base = pl.multiple_of(pl.program_id(0) * TY, TY)
    for x in range(CX):
        curve = laplacian(x, src, lo, hi, pad)
        lap[x] = curve
        here = src[x, pl.ds(base, TY), :]
        new[x] = 2.0 * here - old[x] + c[x] * c[x] * curve
    add_source(new, cells, amps[step], (nlo, nhi))


def last_forward_kernel(step, cells, amps, src, lo, hi, old, c, q4, img, new, grad, pad):
    fill_pad(src, pad)
    base = pl.multiple_of(pl.program_id(0) * TY, TY)
    for x in range(CX):
        curve = laplacian(x, src, lo, hi, pad)
        here = src[x, pl.ds(base, TY), :]
        new[x] = 2.0 * here - old[x] + c[x] * c[x] * curve
        grad[x] = 2.0 * c[x] * (img[x] + q4[x] * curve)
    add_source(new, cells, amps[step], None)


def residual_term(step, x, res):
    lane = lax.broadcasted_iota(jnp.int32, (TY, AZ), 1)
    at = step * CX + x
    rows = res[...]
    if at:
        rows = pltpu.roll(rows, AZ - at, 1)
    return jnp.where(lane == 0, rows, 0.0)


def adjoint_kernel(step, src, lo, hi, now, old, c, res, new, u, ulo, uhi, pad):
    fill_pad(src, pad)
    for x in range(CX):
        value = 2.0 * now[x] - old[x] + laplacian(x, src, lo, hi, pad)
        value = value + residual_term(step, x, res)
        new[x] = value
        u[x] = c[x] * c[x] * value
    ulo[...] = u[0:R]
    uhi[...] = u[CX - R :]


def image_kernel(
    step, src, lo, hi, now, old, c, res, q3, lap2, lap1, lap0, new, u, ulo, uhi, img, pad
):
    adjoint_kernel(step, src, lo, hi, now, old, c, res, new, u, ulo, uhi, pad)
    for x in range(CX):
        img[x] = q3[x] * lap2[x] + now[x] * lap1[x] + new[x] * lap0[x]


def last_adjoint_kernel(step, src, lo, hi, now, old, res, new, pad):
    fill_pad(src, pad)
    for x in range(CX):
        value = 2.0 * now[x] - old[x] + laplacian(x, src, lo, hi, pad)
        new[x] = value + residual_term(step, x, res)


PAD_SCRATCH = pltpu.VMEM((CX, AY + 2 * PAD, AZ), F32)
RES = pl.BlockSpec((TY, AZ), lambda i, *_: (i, 0))


def run(kernel, scalars, args, in_specs, outs, stencil=True, flops=10_000_000):
    shapes = {"s": (SLAB, BLOCK), "h": (HALO, HBLOCK)}
    kinds = [shapes[k] for k in outs]
    traffic = sum(a.size * 4 for a in args) + sum(4 * s[0] * s[1] * s[2] for s, _ in kinds)
    return pl.pallas_call(
        kernel,
        grid_spec=pltpu.PrefetchScalarGridSpec(
            num_scalar_prefetch=len(scalars),
            grid=(KY,),
            in_specs=in_specs,
            out_specs=[b for _, b in kinds],
            scratch_shapes=[PAD_SCRATCH] if stencil else [],
        ),
        out_shape=[sds(s) for s, _ in kinds],
        compiler_params=pltpu.CompilerParams(vmem_limit_bytes=VMEM),
        cost_estimate=pl.CostEstimate(flops=flops, bytes_accessed=traffic, transcendentals=0),
    )(*scalars, *args)


STENCIL = [WHOLE, HBLOCK, HBLOCK]


def pick_kernel(which, slot, b0, b1, b2, b3, out, sem):
    bufs = (b0, b1, b2, b3)
    for i in range(KY):
        for b in range(N_SHOT):

            @pl.when(which[i] == b)
            def _():
                pltpu.make_async_copy(
                    bufs[b].at[slot[i]], out.at[:, pl.ds(i * TY, TY), :], sem.at[i]
                ).start()

    for i in range(KY):
        pltpu.make_async_copy(
            b0.at[slot[i]], out.at[:, pl.ds(i * TY, TY), :], sem.at[i]
        ).wait()


def pick_tiles(which, slot, bufs):
    return pl.pallas_call(
        pick_kernel,
        grid_spec=pltpu.PrefetchScalarGridSpec(
            num_scalar_prefetch=2,
            grid=(1,),
            in_specs=[pl.BlockSpec(memory_space=pl.ANY)] * 4,
            out_specs=pl.BlockSpec(memory_space=pl.ANY),
            scratch_shapes=[pltpu.SemaphoreType.DMA((KY,))],
        ),
        out_shape=sds(SLAB),
    )(which, slot, *bufs)


def pack_kernel(tile_of, slab, o0, o1, o2, o3, sem):
    outs = (o0, o1, o2, o3)
    copies = []
    for b in range(N_SHOT):
        for k in range(SHARE):
            n = b * SHARE + k
            start = pl.multiple_of(tile_of[n] * TY, TY)
            copies.append(
                pltpu.make_async_copy(slab.at[:, pl.ds(start, TY), :], outs[b].at[k], sem.at[n])
            )
    for copy in copies:
        copy.start()
    for copy in copies:
        copy.wait()


def pack_tiles(tile_of, slab):
    part = sds((SHARE, CX, TY, AZ))
    return pl.pallas_call(
        pack_kernel,
        grid_spec=pltpu.PrefetchScalarGridSpec(
            num_scalar_prefetch=1,
            grid=(1,),
            in_specs=[pl.BlockSpec(memory_space=pl.ANY)],
            out_specs=[pl.BlockSpec(memory_space=pl.ANY)] * 4,
            scratch_shapes=[pltpu.SemaphoreType.DMA((N_SHOT * SHARE,))],
        ),
        out_shape=[part] * 4,
    )(tile_of, slab)


def merge_kernel(used, b0, b1, b2, b3, out):
    slot = pl.program_id(0)
    bufs = (b0, b1, b2, b3)
    for half in range(2):
        total = jnp.zeros((CX, TY, AZ), F32)
        for b in range(N_SHOT):
            total = total + jnp.where(used[(b * SHARE + slot) * 2 + half] == 1, bufs[b][0], 0.0)
        out[half, 0] = total


def merge_tiles(used, bufs):
    spec = pl.BlockSpec((1, CX, TY, AZ), lambda k, *_: (k, 0, 0, 0))
    return pl.pallas_call(
        merge_kernel,
        grid_spec=pltpu.PrefetchScalarGridSpec(
            num_scalar_prefetch=1,
            grid=(SHARE,),
            in_specs=[spec] * 4,
            out_specs=pl.BlockSpec((2, 1, CX, TY, AZ), lambda k, *_: (0, k, 0, 0, 0)),
        ),
        out_shape=sds((2, SHARE, CX, TY, AZ)),
        compiler_params=pltpu.CompilerParams(vmem_limit_bytes=VMEM),
    )(used, *bufs)


def within_shots(value, flip):
    return lax.ppermute(value, "shot", [(s, s ^ flip) for s in range(N_SHOT)])


def shift_shot(value, shot, steps):
    pairs = []
    for s in range(N_SHOT):
        for j in range(N_SUB):
            to = (j + steps) % N_SUB if s == shot else j
            pairs.append((s * N_SUB + j, s * N_SUB + to))
    return lax.ppermute(value, ("shot", "sub"), pairs)


def shift_all(value, amounts, sign):
    for shot in range(N_SHOT):
        branches = [lambda v: v]
        for k in range(1, N_SUB):
            branches.append(functools.partial(shift_shot, shot=shot, steps=sign * k))
        value = lax.switch(amounts[shot], branches, value)
    return value


def exchange(low_planes, high_planes, my_sub):
    up = [(i, i + 1) for i in range(N_SUB - 1)]
    down = [(b, a) for a, b in up]
    before = lax.ppermute(high_planes, "sub", up)
    after = lax.ppermute(low_planes, "sub", down)
    return before, after


def body(
    courant_tiles,
    tile_place,
    anchors,
    source_cells,
    wavelet,
    forward_state,
    adjoint_state,
    residual,
):
    my_shot = lax.axis_index("shot")
    my_sub = lax.axis_index("sub")
    start_x = anchors[:, 0]
    start_y = anchors[:, 1]
    amounts = start_x % N_SUB
    upper = (my_sub < start_x).astype(jnp.int32)
    column = my_sub + upper * N_SUB
    ids = start_y[:, None] + jnp.arange(KY, dtype=jnp.int32)[None, :]
    places = tile_place[column[:, None], ids]
    own_places = places[my_shot]

    pm, p0 = forward_state[0, 0], forward_state[0, 1]
    q5, q4 = adjoint_state[0, 0], adjoint_state[0, 1]

    bufs = []
    for flip in range(N_SHOT):
        mine = lax.dynamic_slice_in_dim(courant_tiles, upper[my_shot ^ flip] * SHARE, SHARE, 0)
        bufs.append(within_shots(mine, flip) if flip else mine)
    which = (own_places // SHARE) ^ my_shot
    slot = own_places % SHARE
    before, after = exchange(p0[0:R], p0[CX - R :], my_sub)
    slab = pick_tiles(which, slot, bufs)
    (lap0,) = run(lap_kernel, (), (p0, before, after), STENCIL, "s")
    c = shift_all(slab, amounts, -1)

    cells = source_cells[my_shot] - jnp.stack([my_sub * CX, 0, 0]).astype(jnp.int32)
    amps = wavelet[0]
    res = jnp.pad(
        residual[0].reshape(STEPS * CX, AY).T, ((0, 0), (0, AZ - STEPS * CX))
    )

    p1, plo, phi, u, ulo, uhi = run(
        first_kernel, (cells, amps), (p0, pm, lap0, c, q4), [BLOCK] * 5, "shhshh", stencil=False
    )
    ub, ua = exchange(ulo, uhi, my_sub)
    pb, pa = exchange(plo, phi, my_sub)
    q3, u, ulo, uhi = run(
        functools.partial(adjoint_kernel, 0),
        (),
        (u, ub, ua, q4, q5, c, res),
        STENCIL + [BLOCK] * 3 + [RES],
        "sshh",
    )
    ub, ua = exchange(ulo, uhi, my_sub)
    lap1, p2, plo, phi = run(
        functools.partial(forward_kernel, 1),
        (cells, amps),
        (p1, pb, pa, p0, c),
        STENCIL + [BLOCK] * 2,
        "sshh",
    )
    pb, pa = exchange(plo, phi, my_sub)
    q2, u, ulo, uhi = run(
        functools.partial(adjoint_kernel, 1),
        (),
        (u, ub, ua, q3, q4, c, res),
        STENCIL + [BLOCK] * 3 + [RES],
        "sshh",
    )
    ub, ua = exchange(ulo, uhi, my_sub)
    lap2, p3, plo, phi = run(
        functools.partial(forward_kernel, 2),
        (cells, amps),
        (p2, pb, pa, p1, c),
        STENCIL + [BLOCK] * 2,
        "sshh",
    )
    pb, pa = exchange(plo, phi, my_sub)
    q1, u, ulo, uhi, img = run(
        functools.partial(image_kernel, 2),
        (),
        (u, ub, ua, q2, q3, c, res, q3, lap2, lap1, lap0),
        STENCIL + [BLOCK] * 3 + [RES] + [BLOCK] * 4,
        "sshhs",
    )
    ub, ua = exchange(ulo, uhi, my_sub)
    p4, grad = run(
        functools.partial(last_forward_kernel, 3),
        (cells, amps),
        (p3, pb, pa, p2, c, q4, img),
        STENCIL + [BLOCK] * 4,
        "ss",
    )
    (q0,) = run(
        functools.partial(last_adjoint_kernel, 3),
        (),
        (u, ub, ua, q1, q2, res),
        STENCIL + [BLOCK] * 2 + [RES],
        "s",
    )

    back = shift_all(grad, amounts, 1)
    holder = jnp.arange(N_SHOT, dtype=jnp.int32)[:, None] ^ my_shot
    spot = holder * SHARE + jnp.arange(SHARE, dtype=jnp.int32)[None, :]
    match = spot.reshape(-1)[:, None] == own_places[None, :]
    tile_of = jnp.sum(
        jnp.where(match, jnp.arange(KY, dtype=jnp.int32)[None, :], 0), axis=1, dtype=jnp.int32
    )
    parts = pack_tiles(tile_of, back)
    got = [within_shots(part, flip) if flip else part for flip, part in enumerate(parts)]
    source = jnp.arange(N_SHOT, dtype=jnp.int32) ^ my_shot
    mine = my_shot * SHARE + jnp.arange(SHARE, dtype=jnp.int32)
    covered = jnp.any(places[source][:, None, :] == mine[None, :, None], axis=2)
    side = upper[source][:, None, None] == jnp.arange(2, dtype=jnp.int32)[None, None, :]
    used = (covered[:, :, None] & side).astype(jnp.int32).reshape(-1)
    gradient_tiles = merge_tiles(used, got).reshape(courant_tiles.shape)

    return (jnp.stack([p3, p4])[None], jnp.stack([q1, q0])[None], gradient_tiles)


def solution(mesh):
    return jax.shard_map(
        body,
        mesh=mesh,
        in_specs=(
            P(("shot", "sub"), None, None, None),
            P(),
            P(),
            P(),
            P("shot", None),
            P("shot", None, "sub", None, None),
            P("shot", None, "sub", None, None),
            P("shot", None, "sub", None),
        ),
        out_specs=(
            P("shot", None, "sub", None, None),
            P("shot", None, "sub", None, None),
            P(("shot", "sub"), None, None, None),
        ),
        check_vma=False,
    )
```

time: 736 us -> 479 us (0.65); the launches traced: 722 us -> 489 us
  other arithmetic: 247 us -> 8.47 us
  waiting for transfers between devices: 308 us -> 78.7 us
  Pallas kernels: 0 us -> 168 us
  starting transfers between devices: 96.2 us -> 179 us
  between operations: 17.7 us -> 6.49 us
    add x11 -> x3, other arithmetic: 180 us -> 1.19 us  [the longest x1 0.64 us: body(): spot = holder * SHARE + jnp.arange(SHARE, dtype=jnp.int32)[None, :]]
    pallas_call x0 -> x12, Pallas kernels: none -> 168 us  [the longest x1 73.5 us: pack_tiles(): pl.pallas_call(pack_kernel, grid_spec=pltpu.PrefetchScalarGridSpec(num_sc...]
    ppermute x26, waiting for transfers between devices: 228 us -> 78.7 us  [the longest x4 37.8 us: shift_shot(): return lax.ppermute(value, ('shot', 'sub'), pairs)]
    ppermute x26, starting transfers between devices: 96.1 us -> 179 us  [the longest x6 72.9 us: within_shots(): return lax.ppermute(value, 'shot', [(s, s ^ flip) for s in range(N_SHOT)])]
    all_gather x1 -> x0, waiting for transfers between devices: 53.9 us -> none  [body(): gathered = lax.all_gather(courant_tiles, 'shot', axis=0, tiled=True)]
    concatenate x9 -> x1, other arithmetic: 41.5 us -> 0.07 us  [body(): places = tile_place[column[:, None], ids]]
    reduce_scatter x1 -> x0, waiting for transfers between devices: 25.3 us -> none  [body(): lax.psum_scatter(spread, 'shot', scatter_dimension=0, tiled=True)]
    unnamed x53 -> x97, local copies, waits for them, and re-layouts: 6.1 us -> 29.4 us
  transfers between devices with their start and end apart: 28 -> 26, of which waited for: 14 -> 9; matrix products, arithmetic and copies ran while one was open for 37% -> 4% of each run, Pallas kernels for 0% -> 32%
where the time goes in v1:
time: 479 us; the launch traced here: 489 us
  starting transfers between devices  179 us (37%)
  Pallas kernels  168 us (35%)
  waiting for transfers between devices  78.7 us (16%)
  local copies, waits for them, and re-layouts  46.8 us (10%)
  other arithmetic  8.47 us (2%)
  between operations  6.49 us (1%)
    pallas_call x1, Pallas kernels, pack_tiles(): pl.pallas_call(pack_kernel, grid_spec=pltpu.PrefetchScalarGridSpec(num_sc...  73.5 us
    ppermute x6, starting transfers between devices, within_shots(): return lax.ppermute(value, 'shot', [(s, s ^ flip) for s in range(N_SHOT)])  72.9 us
    ppermute x4, starting transfers between devices, shift_shot(): return lax.ppermute(value, ('shot', 'sub'), pairs)  55.4 us
    pallas_call x9, Pallas kernels, run(): pl.pallas_call(kernel, grid_spec=pltpu.PrefetchScalarGridSpec(num_scalar_...  53.1 us
    ppermute x8, starting transfers between devices, exchange(): before = lax.ppermute(high_planes, 'sub', up)  40.2 us
    ppermute x4, waiting for transfers between devices, shift_shot(): return lax.ppermute(value, ('shot', 'sub'), pairs)  37.8 us
    pallas_call x1, Pallas kernels, pick_tiles(): pl.pallas_call(pick_kernel, grid_spec=pltpu.PrefetchScalarGridSpec(num_sc...  37.6 us
    unnamed x97, local copies, waits for them, and re-layouts  29.4 us
  transfers between devices with their start and end apart: 26, of which 9 were waited for; matrix products, arithmetic and copies ran while one was open for 4% of the time, Pallas kernels for 32%

profile of v1, /device:TPU:1, one launch (start us, length us, event | category | flops | bytes accessed | tf_op | source)
XLA Modules:
  0.0 488.6 jit_solution(12528476761247929250)
XLA Ops:
  4.7 5.5 %collective-permute-start.248 = (f32[4,384,128]{2,1,0:T(8,128)}, f32[4,384,128]{2,1,0:T(8,128)}, u32[]{:S(2)}, u32[]{:S(2)}) collective-permute-start(f32[4,384,128]{2,1,0:T(8,128)} %get-tuple-element.594), channel_id=1, source_target_pairs={{0,1},{1,2},{2,3},{3,4},{4,5},{5,6},{6,7},{7,8},{8,9},{9,10},{10,1... | collective-permute-start | bytes 2359304 | tf_op jit(solution)/shard_map/ppermute | solution.py:299
  14.9 14.0 %collective-permute-start.252 = (f32[3,6,64,128]{3,2,1,0:T(8,128)}, f32[3,6,64,128]{3,2,1,0:T(8,128)}, u32[]{:S(2)}, u32[]{:S(2)}) collective-permute-start(f32[3,6,64,128]{3,2,1,0:T(8,128)} %get-tuple-element.597), channel_id=1, source_target_pairs={{0,96},{32,64},{64,32},{96,0},{1,97},{33,65},{65,33},{97,1},{2,98}... | collective-permute-start | bytes 1769480 | tf_op jit(solution)/shard_map/ppermute | solution.py:275
  28.9 8.9 %collective-permute-start.250 = (f32[3,6,64,128]{3,2,1,0:T(8,128)}, f32[3,6,64,128]{3,2,1,0:T(8,128)}, u32[]{:S(2)}, u32[]{:S(2)}) collective-permute-start(f32[3,6,64,128]{3,2,1,0:T(8,128)} %get-tuple-element.598), channel_id=1, source_target_pairs={{0,32},{32,0},{64,96},{96,64},{1,33},{33,1},{65,97},{97,65},{2,34}... | collective-permute-start | bytes 1769480 | tf_op jit(solution)/shard_map/ppermute | solution.py:275
  37.8 8.9 %collective-permute-start.251 = (f32[3,6,64,128]{3,2,1,0:T(8,128)}, f32[3,6,64,128]{3,2,1,0:T(8,128)}, u32[]{:S(2)}, u32[]{:S(2)}) collective-permute-start(f32[3,6,64,128]{3,2,1,0:T(8,128)} %get-tuple-element.600), channel_id=1, source_target_pairs={{0,64},{32,96},{64,0},{96,32},{1,65},{33,97},{65,1},{97,33},{2,66}... | collective-permute-start | bytes 1769480 | tf_op jit(solution)/shard_map/ppermute | solution.py:275
  56.9 5.0 %collective-permute-done.251.b2 = f32[3,6,64,128]{3,2,1,0:T(8,128)} collective-permute-done((f32[3,6,64,128]{3,2,1,0:T(8,128)}, f32[3,6,64,128]{3,2,1,0:T(8,128)}, u32[]{:S(2)}, u32[]{:S(2)}) %collective-permute-start.251) | collective-permute-done | bytes 589856 | tf_op jit(solution)/shard_map/ppermute | solution.py:275
  61.9 37.6 %shard_map.104 = f32[6,384,128]{2,1,0:T(8,128)} custom-call(s32[6]{0:T(128)} %fusion.12.which, s32[6]{0:T(128)} %get-tuple-element.589.slot, f32[3,6,64,128]{3,2,1,0:T(8,128)} %get-tuple-element.599.b0, f32[3,6,64,128]{3,2,1,0:T(8,128)} %collective-permute-done.250.b1, f32[3,6,64,128]{3,2,1,0:T(8,128)} %collective-permute-done.251.b2, ...), custom_call_target="tpu_custom_call" | custom-call | tf_op jit(solution)/shard_map/pallas_call | solution.py:205
  99.6 33.5 %conditional.9 = (f32[6,384,128]{2,1,0:T(8,128)}) conditional(s32[]{:T(128)} %bitcast.10, f32[6,384,128]{2,1,0:T(8,128)} %get-tuple-element.614, f32[6,384,128]{2,1,0:T(8,128)} %get-tuple-element.614, f32[6,384,128]{2,1,0:T(8,128)} %get-tuple-element.614, f32[6,384,128]{2,1,0:T(8,128)} %get-tuple-element.614, ...), branch_computations={%region_32.33_spmd, %region_33.34_spmd, %region_34.35_spmd, %regio... | conditional | bytes 7077936 | solution.py:292
  99.6 10.3 %collective-permute-start.53 = (f32[6,384,128]{2,1,0:T(8,128)}, f32[6,384,128]{2,1,0:T(8,128)S(1)}, u32[]{:S(2)}, u32[]{:S(2)}) collective-permute-start(f32[6,384,128]{2,1,0:T(8,128)} %param.55), channel_id=1, source_target_pairs={{0,0},{1,1},{2,2},{3,3},{4,4},{5,5},{6,6},{7,7},{8,8},{9,9},{10,10... | collective-permute-start | bytes 3538952 | tf_op jit(solution)/shard_map/cond/branch_23_fun/ppermute | solution.py:284
  110.0 21.8 %collective-permute-done.53 = f32[6,384,128]{2,1,0:T(8,128)S(1)} collective-permute-done((f32[6,384,128]{2,1,0:T(8,128)}, f32[6,384,128]{2,1,0:T(8,128)S(1)}, u32[]{:S(2)}, u32[]{:S(2)}) %collective-permute-start.53) | collective-permute-done | bytes 1179680 | tf_op jit(solution)/shard_map/cond/branch_23_fun/ppermute | solution.py:284
  137.3 5.3 %shard_map.103.lap.lap0 = f32[6,384,128]{2,1,0:T(8,128)S(1)} custom-call(f32[6,384,128]{2,1,0:T(8,128)S(1)} %get-tuple-element.612.src.p0.old, f32[4,384,128]{2,1,0:T(8,128)} %collective-permute-done.248.lo, f32[4,384,128]{2,1,0:T(8,128)} %collective-permute-done.249.hi), custom_call_target="tpu_custom_call" | custom-call | flops 10000000 | bytes 3932160 | tf_op jit(solution)/shard_map/pallas_call | solution.py:169
  153.1 4.9 collective-permute-start.253
  159.5 9.1 %collective-permute-done.259.lo = f32[4,384,128]{2,1,0:T(8,128)S(1)} collective-permute-done((f32[4,384,128]{2,1,0:T(8,128)}, f32[4,384,128]{2,1,0:T(8,128)S(1)}, u32[]{:S(2)}, u32[]{:S(2)}) %collective-permute-start.259) | collective-permute-done | bytes 786464 | tf_op jit(solution)/shard_map/ppermute | solution.py:299
  176.1 5.8 %shard_map.108 = (f32[6,384,128]{2,1,0:T(8,128)S(1)}, f32[6,384,128]{2,1,0:T(8,128)S(1)}, f32[4,384,128]{2,1,0:T(8,128)S(1)}, f32[4,384,128]{2,1,0:T(8,128)S(1)}) custom-call(f32[6,384,128]{2,1,0:T(8,128)S(1)} %copy-done.25, f32[4,384,128]{2,1,0:T(8,128)S(1)} %copy-done.35, f32[4,384,128]{2,1,0:T(8,128)} %collective-permute-done.260.hi, ...), custom_call_target="tpu_custom_call" | custom-call | flops 10000000 | bytes 10420224 | tf_op jit(solution)/shard_map/pallas_call | solution.py:169
  189.3 7.0 %shard_map.106 = (f32[6,384,128]{2,1,0:T(8,128)S(1)}, f32[6,384,128]{2,1,0:T(8,128)S(1)}, f32[4,384,128]{2,1,0:T(8,128)}, f32[4,384,128]{2,1,0:T(8,128)}) custom-call(s32[3]{0:T(128)S(1)} %fusion.4.cells, f32[4]{0:T(128)S(1)} %bitcast.55, f32[6,384,128]{2,1,0:T(8,128)S(1)} %copy-done.20, f32[4,384,128]{2,1,0:T(8,128)} %collective-permute-done.253.lo, ...), custom_call_target="tpu_custom_call" | custom-call | flops 10000000 | bytes 9043968 | tf_op jit(solution)/shard_map/pallas_call | solution.py:169
  205.5 5.0 %shard_map.109 = (f32[6,384,128]{2,1,0:T(8,128)S(1)}, f32[6,384,128]{2,1,0:T(8,128)S(1)}, f32[4,384,128]{2,1,0:T(8,128)}, f32[4,384,128]{2,1,0:T(8,128)}) custom-call(f32[6,384,128]{2,1,0:T(8,128)S(1)} %get-tuple-element.568.src, f32[4,384,128]{2,1,0:T(8,128)S(1)} %collective-permute-done.261.lo, f32[4,384,128]{2,1,0:T(8,128)S(1)} %collective-permute-done.262.hi, ...), custom_call_target="tpu_custom_call" | custom-call | flops 10000000 | bytes 10420224 | tf_op jit(solution)/shard_map/pallas_call | solution.py:169
  212.6 6.9 %collective-permute-start.263 = (f32[4,384,128]{2,1,0:T(8,128)}, f32[4,384,128]{2,1,0:T(8,128)}, u32[]{:S(2)}, u32[]{:S(2)}) collective-permute-start(f32[4,384,128]{2,1,0:T(8,128)} %get-tuple-element.573), channel_id=1, source_target_pairs={{0,1},{1,2},{2,3},{3,4},{4,5},{5,6},{6,7},{7,8},{8,9},{9,10},{10,1... | collective-permute-start | bytes 2359304 | tf_op jit(solution)/shard_map/ppermute | solution.py:299
  225.4 7.1 %shard_map.107 = (f32[6,384,128]{2,1,0:T(8,128)S(1)}, f32[6,384,128]{2,1,0:T(8,128)S(1)}, f32[4,384,128]{2,1,0:T(8,128)}, f32[4,384,128]{2,1,0:T(8,128)}) custom-call(s32[3]{0:T(128)S(1)} %fusion.4.cells, f32[4]{0:T(128)S(1)} %bitcast.56, f32[6,384,128]{2,1,0:T(8,128)S(1)} %copy-done.17, f32[4,384,128]{2,1,0:T(8,128)S(1)} %copy-done.37, ...), custom_call_target="tpu_custom_call" | custom-call | flops 10000000 | bytes 9043968 | tf_op jit(solution)/shard_map/pallas_call | solution.py:169
  234.5 9.3 %collective-permute-start.257 = (f32[4,384,128]{2,1,0:T(8,128)}, f32[4,384,128]{2,1,0:T(8,128)}, u32[]{:S(2)}, u32[]{:S(2)}) collective-permute-start(f32[4,384,128]{2,1,0:T(8,128)} %get-tuple-element.563), channel_id=1, source_target_pairs={{0,1},{1,2},{2,3},{3,4},{4,5},{5,6},{6,7},{7,8},{8,9},{9,10},{10,1... | collective-permute-start | bytes 2359304 | tf_op jit(solution)/shard_map/ppermute | solution.py:299
  253.7 6.8 %shard_map.110 = (f32[6,384,128]{2,1,0:T(8,128)S(1)}, f32[6,384,128]{2,1,0:T(8,128)S(1)}, f32[4,384,128]{2,1,0:T(8,128)}, f32[4,384,128]{2,1,0:T(8,128)}, f32[6,384,128]{2,1,0:T(8,128)S(1)}) custom-call(f32[6,384,128]{2,1,0:T(8,128)S(1)} %copy-done.29, f32[4,384,128]{2,1,0:T(8,128)} %collective-permute-done.263.lo, ...), custom_call_target="tpu_custom_call" | custom-call | flops 10000000 | bytes 16318464 | tf_op jit(solution)/shard_map/pallas_call | solution.py:169
  275.9 7.1 %shard_map.111 = (f32[6,384,128]{2,1,0:T(8,128)S(1)}, f32[6,384,128]{2,1,0:T(8,128)}) custom-call(s32[3]{0:T(128)S(1)} %fusion.4.cells, f32[4]{0:T(128)S(1)} %bitcast.57, f32[6,384,128]{2,1,0:T(8,128)S(1)} %copy-done.14, f32[4,384,128]{2,1,0:T(8,128)} %collective-permute-done.257.lo, f32[4,384,128]{2,1,0:T(8,128)} %collective-permute-done.258.hi, ...), custom_call_target="tpu_custom_call" | custom-call | flops 10000000 | bytes 9830400 | tf_op jit(solution)/shard_map/pallas_call | solution.py:169
  283.0 49.5 %conditional.13 = (f32[6,384,128]{2,1,0:T(8,128)}) conditional(s32[]{:T(128)} %bitcast.10, f32[6,384,128]{2,1,0:T(8,128)} %get-tuple-element.618, f32[6,384,128]{2,1,0:T(8,128)} %get-tuple-element.618, f32[6,384,128]{2,1,0:T(8,128)} %get-tuple-element.618, f32[6,384,128]{2,1,0:T(8,128)} %get-tuple-element.618, ...), branch_computations={%region_162.163_spmd, %region_163.164_spmd, %region_164.165_spmd, ... | conditional | bytes 7077936 | solution.py:292
  283.2 32.1 %collective-permute-start.177 = (f32[6,384,128]{2,1,0:T(8,128)}, f32[6,384,128]{2,1,0:T(8,128)S(1)}, u32[]{:S(2)}, u32[]{:S(2)}) collective-permute-start(f32[6,384,128]{2,1,0:T(8,128)} %param.183), channel_id=1, source_target_pairs={{0,0},{1,1},{2,2},{3,3},{4,4},{5,5},{6,6},{7,7},{8,8},{9,9},{10,10... | collective-permute-start | bytes 3538952 | tf_op jit(solution)/shard_map/cond/branch_23_fun/ppermute | solution.py:284
  315.3 16.1 %collective-permute-done.177 = f32[6,384,128]{2,1,0:T(8,128)S(1)} collective-permute-done((f32[6,384,128]{2,1,0:T(8,128)}, f32[6,384,128]{2,1,0:T(8,128)S(1)}, u32[]{:S(2)}, u32[]{:S(2)}) %collective-permute-start.177) | collective-permute-done | bytes 1179680 | tf_op jit(solution)/shard_map/cond/branch_23_fun/ppermute | solution.py:284
  332.4 10.9 %conditional.14 = (f32[6,384,128]{2,1,0:T(8,128)}) conditional(s32[]{:T(128)} %bitcast.9, f32[6,384,128]{2,1,0:T(8,128)} %get-tuple-element.619, f32[6,384,128]{2,1,0:T(8,128)} %get-tuple-element.619, f32[6,384,128]{2,1,0:T(8,128)} %get-tuple-element.619, f32[6,384,128]{2,1,0:T(8,128)} %get-tuple-element.619, ...), branch_computations={%region_194.195_spmd, %region_195.196_spmd, %region_196.197_spmd, ... | conditional | bytes 7077936 | solution.py:292
  332.4 9.8 %collective-permute-start.193 = (f32[6,384,128]{2,1,0:T(8,128)}, f32[6,384,128]{2,1,0:T(8,128)S(1)}, u32[]{:S(2)}, u32[]{:S(2)}) collective-permute-start(f32[6,384,128]{2,1,0:T(8,128)} %param.200), channel_id=1, source_target_pairs={{0,0},{1,1},{2,2},{3,3},{4,4},{5,5},{6,6},{7,7},{8,8},{9,9},{10,10... | collective-permute-start | bytes 3538952 | tf_op jit(solution)/shard_map/cond/branch_8_fun/ppermute | solution.py:284
  343.3 73.5 %shard_map.113 = (f32[3,6,64,128]{3,2,1,0:T(8,128)}, f32[3,6,64,128]{3,2,1,0:T(8,128)}, f32[3,6,64,128]{3,2,1,0:T(8,128)}, f32[3,6,64,128]{3,2,1,0:T(8,128)}) custom-call(s32[12]{0:T(128)} %select_reduce_fusion.tile_of, f32[6,384,128]{2,1,0:T(8,128)} %get-tuple-element.621.slab), custom_call_target="tpu_custom_call" | custom-call | tf_op jit(solution)/shard_map/pallas_call | solution.py:236
  416.8 23.3 %collective-permute-start.267 = (f32[3,6,64,128]{3,2,1,0:T(8,128)}, f32[3,6,64,128]{3,2,1,0:T(8,128)}, u32[]{:S(2)}, u32[]{:S(2)}) collective-permute-start(f32[3,6,64,128]{3,2,1,0:T(8,128)} %get-tuple-element.586), channel_id=1, source_target_pairs={{0,32},{32,0},{64,96},{96,64},{1,33},{33,1},{65,97},{97,65},{2,34}... | collective-permute-start | bytes 1769480 | tf_op jit(solution)/shard_map/ppermute | solution.py:275
  440.0 8.9 %collective-permute-start.268 = (f32[3,6,64,128]{3,2,1,0:T(8,128)}, f32[3,6,64,128]{3,2,1,0:T(8,128)}, u32[]{:S(2)}, u32[]{:S(2)}) collective-permute-start(f32[3,6,64,128]{3,2,1,0:T(8,128)} %get-tuple-element.587), channel_id=1, source_target_pairs={{0,64},{32,96},{64,0},{96,32},{1,65},{33,97},{65,1},{97,33},{2,66}... | collective-permute-start | bytes 1769480 | tf_op jit(solution)/shard_map/ppermute | solution.py:275
  448.9 8.9 %collective-permute-start.269 = (f32[3,6,64,128]{3,2,1,0:T(8,128)}, f32[3,6,64,128]{3,2,1,0:T(8,128)}, u32[]{:S(2)}, u32[]{:S(2)}) collective-permute-start(f32[3,6,64,128]{3,2,1,0:T(8,128)} %get-tuple-element.588), channel_id=1, source_target_pairs={{0,96},{32,64},{64,32},{96,0},{1,97},{33,65},{65,33},{97,1},{2,98}... | collective-permute-start | bytes 1769480 | tf_op jit(solution)/shard_map/ppermute | solution.py:275
  459.7 4.4 collective-permute-done.268.b2
  464.2 12.8 %collective-permute-done.269.b3 = f32[3,6,64,128]{3,2,1,0:T(8,128)} collective-permute-done((f32[3,6,64,128]{3,2,1,0:T(8,128)}, f32[3,6,64,128]{3,2,1,0:T(8,128)}, u32[]{:S(2)}, u32[]{:S(2)}) %collective-permute-start.269) | collective-permute-done | bytes 589856 | tf_op jit(solution)/shard_map/ppermute | solution.py:275
  481.3 5.2 %shard_map.112 = f32[6,384,128]{2,1,0:T(8,128)S(1)} custom-call(f32[6,384,128]{2,1,0:T(8,128)S(1)} %copy-done.23, f32[4,384,128]{2,1,0:T(8,128)S(1)} %collective-permute-done.265.lo, f32[4,384,128]{2,1,0:T(8,128)} %collective-permute-done.266.hi, f32[6,384,128]{2,1,0:T(8,128)S(1)} %copy-done.12, f32[6,384,128]{2,1,0:T(8,128)S(1)} %copy-done.10, ...), custom_call_target="tpu_custom_call" | custom-call | flops 10000000 | bytes 6488064 | tf_op jit(solution)/shard_map/pallas_call | solution.py:169
  (174 shorter events, 104.4 us)
Async XLA Ops:
  0.6 48.1 %copy-start = (s32[64,12]{0,1:T(8,128)S(1)}, s32[64,12]{0,1:T(8,128)}, u32[]{:S(2)}) copy-start(s32[64,12]{0,1:T(8,128)} %param.265) | copy-start | bytes 9220
  3.4 133.8 %collective-permute-start.249 = (f32[4,384,128]{2,1,0:T(8,128)}, f32[4,384,128]{2,1,0:T(8,128)}, u32[]{:S(2)}, u32[]{:S(2)}) collective-permute-start(f32[4,384,128]{2,1,0:T(8,128)} %get-tuple-element.593), channel_id=1, source_target_pairs={{1,0},{2,1},{3,2},{4,3},{5,4},{6,5},{7,6},{8,7},{9,8},{10,9},{11,1... | collective-permute-start | bytes 2359304 | tf_op jit(solution)/shard_map/ppermute | solution.py:300
  4.7 132.5 %collective-permute-start.248 = (f32[4,384,128]{2,1,0:T(8,128)}, f32[4,384,128]{2,1,0:T(8,128)}, u32[]{:S(2)}, u32[]{:S(2)}) collective-permute-start(f32[4,384,128]{2,1,0:T(8,128)} %get-tuple-element.594), channel_id=1, source_target_pairs={{0,1},{1,2},{2,3},{3,4},{4,5},{5,6},{6,7},{7,8},{8,9},{9,10},{10,1... | collective-permute-start | bytes 2359304 | tf_op jit(solution)/shard_map/ppermute | solution.py:299
  14.9 42.1 %collective-permute-start.252 = (f32[3,6,64,128]{3,2,1,0:T(8,128)}, f32[3,6,64,128]{3,2,1,0:T(8,128)}, u32[]{:S(2)}, u32[]{:S(2)}) collective-permute-start(f32[3,6,64,128]{3,2,1,0:T(8,128)} %get-tuple-element.597), channel_id=1, source_target_pairs={{0,96},{32,64},{64,32},{96,0},{1,97},{33,65},{65,33},{97,1},{2,98}... | collective-permute-start | bytes 1769480 | tf_op jit(solution)/shard_map/ppermute | solution.py:275
  28.9 28.1 %collective-permute-start.250 = (f32[3,6,64,128]{3,2,1,0:T(8,128)}, f32[3,6,64,128]{3,2,1,0:T(8,128)}, u32[]{:S(2)}, u32[]{:S(2)}) collective-permute-start(f32[3,6,64,128]{3,2,1,0:T(8,128)} %get-tuple-element.598), channel_id=1, source_target_pairs={{0,32},{32,0},{64,96},{96,64},{1,33},{33,1},{65,97},{97,65},{2,34}... | collective-permute-start | bytes 1769480 | tf_op jit(solution)/shard_map/ppermute | solution.py:275
  37.8 24.1 %collective-permute-start.251 = (f32[3,6,64,128]{3,2,1,0:T(8,128)}, f32[3,6,64,128]{3,2,1,0:T(8,128)}, u32[]{:S(2)}, u32[]{:S(2)}) collective-permute-start(f32[3,6,64,128]{3,2,1,0:T(8,128)} %get-tuple-element.600), channel_id=1, source_target_pairs={{0,64},{32,96},{64,0},{96,32},{1,65},{33,97},{65,1},{97,33},{2,66}... | collective-permute-start | bytes 1769480 | tf_op jit(solution)/shard_map/ppermute | solution.py:275
  99.6 32.1 %collective-permute-start.53 = (f32[6,384,128]{2,1,0:T(8,128)}, f32[6,384,128]{2,1,0:T(8,128)S(1)}, u32[]{:S(2)}, u32[]{:S(2)}) collective-permute-start(f32[6,384,128]{2,1,0:T(8,128)} %param.55), channel_id=1, source_target_pairs={{0,0},{1,1},{2,2},{3,3},{4,4},{5,5},{6,6},{7,7},{8,8},{9,9},{10,10... | collective-permute-start | bytes 3538952 | tf_op jit(solution)/shard_map/cond/branch_23_fun/ppermute | solution.py:284
  133.1 3.1 collective-permute-start.69
  148.5 20.1 %collective-permute-start.259 = (f32[4,384,128]{2,1,0:T(8,128)}, f32[4,384,128]{2,1,0:T(8,128)S(1)}, u32[]{:S(2)}, u32[]{:S(2)}) collective-permute-start(f32[4,384,128]{2,1,0:T(8,128)} %get-tuple-element.566), channel_id=1, source_target_pairs={{0,1},{1,2},{2,3},{3,4},{4,5},{5,6},{6,7},{7,8},{8,9},{9,10},{10,1... | collective-permute-start | bytes 2359304 | tf_op jit(solution)/shard_map/ppermute | solution.py:299
  151.8 20.7 %collective-permute-start.260 = (f32[4,384,128]{2,1,0:T(8,128)}, f32[4,384,128]{2,1,0:T(8,128)}, u32[]{:S(2)}, u32[]{:S(2)}) collective-permute-start(f32[4,384,128]{2,1,0:T(8,128)} %get-tuple-element.567), channel_id=1, source_target_pairs={{1,0},{2,1},{3,2},{4,3},{5,4},{6,5},{7,6},{8,7},{9,8},{10,9},{11,1... | collective-permute-start | bytes 2359304 | tf_op jit(solution)/shard_map/ppermute | solution.py:300
  153.1 33.5 %collective-permute-start.253 = (f32[4,384,128]{2,1,0:T(8,128)}, f32[4,384,128]{2,1,0:T(8,128)}, u32[]{:S(2)}, u32[]{:S(2)}) collective-permute-start(f32[4,384,128]{2,1,0:T(8,128)} %get-tuple-element.557), channel_id=1, source_target_pairs={{0,1},{1,2},{2,3},{3,4},{4,5},{5,6},{6,7},{7,8},{8,9},{9,10},{10,1... | collective-permute-start | bytes 2359304 | tf_op jit(solution)/shard_map/ppermute | solution.py:299
  158.0 31.3 %collective-permute-start.254 = (f32[4,384,128]{2,1,0:T(8,128)}, f32[4,384,128]{2,1,0:T(8,128)}, u32[]{:S(2)}, u32[]{:S(2)}) collective-permute-start(f32[4,384,128]{2,1,0:T(8,128)} %get-tuple-element.558), channel_id=1, source_target_pairs={{1,0},{2,1},{3,2},{4,3},{5,4},{6,5},{7,6},{8,7},{9,8},{10,9},{11,1... | collective-permute-start | bytes 2359304 | tf_op jit(solution)/shard_map/ppermute | solution.py:300
  159.5 46.1 %copy-start.4 = (f32[384,128]{1,0:T(8,128)}, f32[384,128]{1,0:T(8,128)S(1)}, u32[]{:S(2)}) copy-start(f32[384,128]{1,0:T(8,128)S(1)} %pad.5.res) | copy-start | bytes 589828
  182.0 19.7 %collective-permute-start.261 = (f32[4,384,128]{2,1,0:T(8,128)S(1)}, f32[4,384,128]{2,1,0:T(8,128)S(1)}, u32[]{:S(2)}, u32[]{:S(2)}) collective-permute-start(f32[4,384,128]{2,1,0:T(8,128)S(1)} %get-tuple-element.569), channel_id=1, source_target_pairs={{0,1},{1,2},{2,3},{3,4},{4,5},{5,6},{6,7},{7,8},{8,9},{9,10},{10,1... | collective-permute-start | bytes 2359304 | tf_op jit(solution)/shard_map/ppermute | solution.py:299
  185.2 20.3 %collective-permute-start.262 = (f32[4,384,128]{2,1,0:T(8,128)S(1)}, f32[4,384,128]{2,1,0:T(8,128)S(1)}, u32[]{:S(2)}, u32[]{:S(2)}) collective-permute-start(f32[4,384,128]{2,1,0:T(8,128)S(1)} %get-tuple-element.570), channel_id=1, source_target_pairs={{1,0},{2,1},{3,2},{4,3},{5,4},{6,5},{7,6},{8,7},{9,8},{10,9},{11,1... | collective-permute-start | bytes 2359304 | tf_op jit(solution)/shard_map/ppermute | solution.py:300
  197.3 23.5 %collective-permute-start.255 = (f32[4,384,128]{2,1,0:T(8,128)}, f32[4,384,128]{2,1,0:T(8,128)S(1)}, u32[]{:S(2)}, u32[]{:S(2)}) collective-permute-start(f32[4,384,128]{2,1,0:T(8,128)} %get-tuple-element.560), channel_id=1, source_target_pairs={{0,1},{1,2},{2,3},{3,4},{4,5},{5,6},{6,7},{7,8},{8,9},{9,10},{10,1... | collective-permute-start | bytes 2359304 | tf_op jit(solution)/shard_map/ppermute | solution.py:299
  200.4 21.4 %collective-permute-start.256 = (f32[4,384,128]{2,1,0:T(8,128)}, f32[4,384,128]{2,1,0:T(8,128)}, u32[]{:S(2)}, u32[]{:S(2)}) collective-permute-start(f32[4,384,128]{2,1,0:T(8,128)} %get-tuple-element.561), channel_id=1, source_target_pairs={{1,0},{2,1},{3,2},{4,3},{5,4},{6,5},{7,6},{8,7},{9,8},{10,9},{11,1... | collective-permute-start | bytes 2359304 | tf_op jit(solution)/shard_map/ppermute | solution.py:300
  212.6 35.0 %collective-permute-start.263 = (f32[4,384,128]{2,1,0:T(8,128)}, f32[4,384,128]{2,1,0:T(8,128)}, u32[]{:S(2)}, u32[]{:S(2)}) collective-permute-start(f32[4,384,128]{2,1,0:T(8,128)} %get-tuple-element.573), channel_id=1, source_target_pairs={{0,1},{1,2},{2,3},{3,4},{4,5},{5,6},{6,7},{7,8},{8,9},{9,10},{10,1... | collective-permute-start | bytes 2359304 | tf_op jit(solution)/shard_map/ppermute | solution.py:299
  219.5 28.1 %collective-permute-start.264 = (f32[4,384,128]{2,1,0:T(8,128)}, f32[4,384,128]{2,1,0:T(8,128)}, u32[]{:S(2)}, u32[]{:S(2)}) collective-permute-start(f32[4,384,128]{2,1,0:T(8,128)} %get-tuple-element.574), channel_id=1, source_target_pairs={{1,0},{2,1},{3,2},{4,3},{5,4},{6,5},{7,6},{8,7},{9,8},{10,9},{11,1... | collective-permute-start | bytes 2359304 | tf_op jit(solution)/shard_map/ppermute | solution.py:300
  225.4 19.7 %copy-start.45 = (s32[4]{0:T(128)S(1)}, s32[4]{0:T(128)}, u32[]{:S(2)}) copy-start(s32[4]{0:T(128)} %get-tuple-element.611) | copy-start | bytes 52
  225.4 22.2 %copy-start.3 = (f32[6,384,128]{2,1,0:T(8,128)S(1)}, f32[6,384,128]{2,1,0:T(8,128)}, u32[]{:S(2)}) copy-start(f32[6,384,128]{2,1,0:T(8,128)} %copy-done.2) | copy-start | bytes 3538948
  234.5 37.5 %collective-permute-start.257 = (f32[4,384,128]{2,1,0:T(8,128)}, f32[4,384,128]{2,1,0:T(8,128)}, u32[]{:S(2)}, u32[]{:S(2)}) collective-permute-start(f32[4,384,128]{2,1,0:T(8,128)} %get-tuple-element.563), channel_id=1, source_target_pairs={{0,1},{1,2},{2,3},{3,4},{4,5},{5,6},{6,7},{7,8},{8,9},{9,10},{10,1... | collective-permute-start | bytes 2359304 | tf_op jit(solution)/shard_map/ppermute | solution.py:299
  243.8 28.2 %collective-permute-start.258 = (f32[4,384,128]{2,1,0:T(8,128)}, f32[4,384,128]{2,1,0:T(8,128)}, u32[]{:S(2)}, u32[]{:S(2)}) collective-permute-start(f32[4,384,128]{2,1,0:T(8,128)} %get-tuple-element.564), channel_id=1, source_target_pairs={{1,0},{2,1},{3,2},{4,3},{5,4},{6,5},{7,6},{8,7},{9,8},{10,9},{11,1... | collective-permute-start | bytes 2359304 | tf_op jit(solution)/shard_map/ppermute | solution.py:300
  263.6 217.7 %collective-permute-start.265 = (f32[4,384,128]{2,1,0:T(8,128)}, f32[4,384,128]{2,1,0:T(8,128)S(1)}, u32[]{:S(2)}, u32[]{:S(2)}) collective-permute-start(f32[4,384,128]{2,1,0:T(8,128)} %get-tuple-element.582), channel_id=1, source_target_pairs={{0,1},{1,2},{2,3},{3,4},{4,5},{5,6},{6,7},{7,8},{8,9},{9,10},{10,1... | collective-permute-start | bytes 2359304 | tf_op jit(solution)/shard_map/ppermute | solution.py:299
  267.7 213.6 %collective-permute-start.266 = (f32[4,384,128]{2,1,0:T(8,128)}, f32[4,384,128]{2,1,0:T(8,128)}, u32[]{:S(2)}, u32[]{:S(2)}) collective-permute-start(f32[4,384,128]{2,1,0:T(8,128)} %get-tuple-element.583), channel_id=1, source_target_pairs={{1,0},{2,1},{3,2},{4,3},{5,4},{6,5},{7,6},{8,7},{9,8},{10,9},{11,1... | collective-permute-start | bytes 2359304 | tf_op jit(solution)/shard_map/ppermute | solution.py:300
  283.2 48.2 %collective-permute-start.177 = (f32[6,384,128]{2,1,0:T(8,128)}, f32[6,384,128]{2,1,0:T(8,128)S(1)}, u32[]{:S(2)}, u32[]{:S(2)}) collective-permute-start(f32[6,384,128]{2,1,0:T(8,128)} %param.183), channel_id=1, source_target_pairs={{0,0},{1,1},{2,2},{3,3},{4,4},{5,5},{6,6},{7,7},{8,8},{9,9},{10,10... | collective-permute-start | bytes 3538952 | tf_op jit(solution)/shard_map/cond/branch_23_fun/ppermute | solution.py:284
  332.4 9.8 %collective-permute-start.193 = (f32[6,384,128]{2,1,0:T(8,128)}, f32[6,384,128]{2,1,0:T(8,128)S(1)}, u32[]{:S(2)}, u32[]{:S(2)}) collective-permute-start(f32[6,384,128]{2,1,0:T(8,128)} %param.200), channel_id=1, source_target_pairs={{0,0},{1,1},{2,2},{3,3},{4,4},{5,5},{6,6},{7,7},{8,8},{9,9},{10,10... | collective-permute-start | bytes 3538952 | tf_op jit(solution)/shard_map/cond/branch_8_fun/ppermute | solution.py:284
  343.3 114.8 %copy-start.15 = (f32[6,384,128]{2,1,0:T(8,128)S(1)}, f32[6,384,128]{2,1,0:T(8,128)}, u32[]{:S(2)}) copy-start(f32[6,384,128]{2,1,0:T(8,128)} %copy-done.13) | copy-start | bytes 3538948
  416.8 43.0 %collective-permute-start.267 = (f32[3,6,64,128]{3,2,1,0:T(8,128)}, f32[3,6,64,128]{3,2,1,0:T(8,128)}, u32[]{:S(2)}, u32[]{:S(2)}) collective-permute-start(f32[3,6,64,128]{3,2,1,0:T(8,128)} %get-tuple-element.586), channel_id=1, source_target_pairs={{0,32},{32,0},{64,96},{96,64},{1,33},{33,1},{65,97},{97,65},{2,34}... | collective-permute-start | bytes 1769480 | tf_op jit(solution)/shard_map/ppermute | solution.py:275
  440.0 24.1 %collective-permute-start.268 = (f32[3,6,64,128]{3,2,1,0:T(8,128)}, f32[3,6,64,128]{3,2,1,0:T(8,128)}, u32[]{:S(2)}, u32[]{:S(2)}) collective-permute-start(f32[3,6,64,128]{3,2,1,0:T(8,128)} %get-tuple-element.587), channel_id=1, source_target_pairs={{0,64},{32,96},{64,0},{96,32},{1,65},{33,97},{65,1},{97,33},{2,66}... | collective-permute-start | bytes 1769480 | tf_op jit(solution)/shard_map/ppermute | solution.py:275
  448.9 28.1 %collective-permute-start.269 = (f32[3,6,64,128]{3,2,1,0:T(8,128)}, f32[3,6,64,128]{3,2,1,0:T(8,128)}, u32[]{:S(2)}, u32[]{:S(2)}) collective-permute-start(f32[3,6,64,128]{3,2,1,0:T(8,128)} %get-tuple-element.588), channel_id=1, source_target_pairs={{0,96},{32,64},{64,32},{96,0},{1,97},{33,65},{65,33},{97,1},{2,98}... | collective-permute-start | bytes 1769480 | tf_op jit(solution)/shard_map/ppermute | solution.py:275
  458.1 23.2 %copy-start.23 = (f32[6,384,128]{2,1,0:T(8,128)S(1)}, f32[6,384,128]{2,1,0:T(8,128)}, u32[]{:S(2)}) copy-start(f32[6,384,128]{2,1,0:T(8,128)} %copy-done.22) | copy-start | bytes 3538948
  (42 other events, 175.4 us)
